TPU v7x, 32 devices: a whole 2x2x4 slice. The times are simulated.
32 devices in a mesh: region: 16 (over z, y, core), obs: 2 (over x).
Axes of the slice: x: 2, y: 2, z: 4, core: 2. Of those that a mesh axis runs over, the one named last changes fastest.
Arguments:
- obs_anomaly: bfloat16 [512, 2048, 128], P('region', 'obs'), may hold values from -1.5 to 1.5
- innovation: bfloat16 [512, 2048], P('region', 'obs'), may hold values from -6 to 6
- obs_count: int32 [512], P('region'), may hold values from 512 to 2048, as said below
- neighbour: int32 [512, 5], P('region'), may hold values from 0 to 511, as said below
- taper: float32 [512, 5], P('region'), may hold values from 0.1 to 1
- param_anomaly: bfloat16 [512, 1024, 128], P('region', 'obs'), may hold values from -6 to 6
- param_mean: float32 [512, 1024], P('region', 'obs'), may hold values from -6 to 6
Outputs:
- analysis: bfloat16 [512, 1024, 128], P('region', 'obs')
Inputs may be any that keep to these rules, and one draw needn't show every extreme that they name: `obs_count`: region 512 counts: some region has all 2048 slots live. neighbour[g, 0] = g; every other entry differs from g cyclically by 1 to 32 regions.
All inputs are finite; a program needn't handle non-finite values.
Results may differ from a plain program's by a relative error of at most 0.013.
Values may be sent and summed in bfloat16 or wider, within the bound.
A program may use at most 192 MiB of HBM per device.

v0:
```python
import jax
import jax.numpy as jnp
from jax import lax
from jax.sharding import PartitionSpec as P


def with_halo(array, sides, width):
    for axis, dim in sides:
        size, length = (lax.axis_size(axis), array.shape[dim])
        up = [(i, (i + 1) % size) for i in range(size)]
        down = [(j, i) for i, j in up]
        last = lax.slice_in_dim(array, length - width, length, axis=dim)
        leading = lax.slice_in_dim(array, 0, width, axis=dim)
        before = lax.ppermute(last, axis, up)
        after = lax.ppermute(leading, axis, down)
        array = jnp.concatenate([before, array, after], axis=dim)
    return array


def lower_inverse(lower):
    width = lower.shape[-1]
    rows = jnp.arange(width, dtype=jnp.int32)[:, None]
    cols = jnp.arange(width, dtype=jnp.int32)[None, :]
    diag = jnp.diagonal(lower, axis1=-2, axis2=-1)
    inverse = jnp.where(rows == cols, (1.0 / diag)[..., None, :], jnp.zeros((), jnp.float32))
    block = 1
    while block < width:
        row_block = rows // block
        col_block = cols // block
        keep = (row_block % 2 == 1) & (col_block == row_block - 1)
        corner = jnp.where(keep, lower, jnp.zeros((), jnp.float32))
        inner = jnp.einsum("bij,bjk->bik", corner, inverse, precision=lax.Precision.HIGHEST)
        inverse = inverse - jnp.einsum(
            "bij,bjk->bik", inverse, inner, precision=lax.Precision.HIGHEST
        )
        block = block * 2
    return inverse


def solve_region(local_gram, local_proj):
    width = local_gram.shape[-1]
    eye = jnp.eye(width, dtype=jnp.float32)
    precision_mat = (width - 1.0) * eye + local_gram
    lower = jnp.linalg.cholesky(precision_mat)
    inverse_lower = lower_inverse(lower)
    step_one = jnp.einsum("bij,bj->bi", inverse_lower, local_proj, precision=lax.Precision.HIGHEST)
    mean_weight = jnp.einsum("bji,bj->bi", inverse_lower, step_one, precision=lax.Precision.HIGHEST)
    spread = jnp.sqrt(width - 1.0) * jnp.swapaxes(inverse_lower, -1, -2)
    return (mean_weight[..., None] + spread).astype(jnp.bfloat16)


def body(obs_anomaly, innovation, obs_count, neighbour, taper, param_anomaly, param_mean):
    regions = obs_anomaly.shape[0]
    slot_count = obs_anomaly.shape[1]
    total = regions * lax.axis_size("region")
    first = lax.axis_index("region") * regions
    slots = lax.axis_index("obs") * slot_count + jnp.arange(slot_count, dtype=jnp.int32)
    live = slots[None, :] < obs_count[:, None]
    masked_y = jnp.where(live[..., None], obs_anomaly, jnp.zeros((), jnp.bfloat16))
    masked_d = jnp.where(live, innovation, jnp.zeros((), jnp.bfloat16))
    position = (neighbour - first + regions) % total
    grams = jnp.einsum("roi,roj->rij", masked_y, masked_y, preferred_element_type=jnp.float32)
    projs = jnp.einsum("roi,ro->ri", masked_y, masked_d, preferred_element_type=jnp.float32)
    wide_g, wide_p = (
        with_halo(grams.astype(jnp.bfloat16), (("region", 0),), regions).astype(grams.dtype),
        with_halo(projs.astype(jnp.bfloat16), (("region", 0),), regions).astype(projs.dtype),
    )
    local_gram = jnp.einsum(
        "rk,rkij->rij", taper, wide_g[position], precision=lax.Precision.HIGHEST
    )
    local_proj = jnp.einsum("rk,rki->ri", taper, wide_p[position], precision=lax.Precision.HIGHEST)
    summed_gram, summed_proj = (
        lax.psum(local_gram.astype(jnp.bfloat16), "obs").astype(jnp.float32),
        lax.psum(local_proj.astype(jnp.bfloat16), "obs").astype(jnp.float32),
    )
    transform = solve_region(summed_gram, summed_proj)
    moved = jnp.einsum("rpk,rkj->rpj", param_anomaly, transform, preferred_element_type=jnp.float32)
    return (param_mean[..., None] + moved).astype(jnp.bfloat16)


def solution(mesh):
    in_specs = (
        P("region", "obs", None),
        P("region", "obs"),
        P("region"),
        P("region", None),
        P("region", None),
        P("region", "obs", None),
        P("region", "obs"),
    )
    out_specs = P("region", "obs", None)
    return jax.shard_map(body, mesh=mesh, in_specs=in_specs, out_specs=out_specs, check_vma=False)
```

profile of v0, /device:TPU:0, one launch (start us, length us, event | category | flops | bytes accessed | tf_op | source)
XLA Modules:
  0.0 610.3 jit_solution(4052308783497451651)
XLA Ops:
  6.5 0.7 broadcast_compare_fusion
  7.3 1.1 select_bitcast_fusion
  8.4 9.0 %fusion = f32[32,1,128]{2,1,0:T(1,128)S(1)} fusion(bf16[32,1024,128]{2,1,0:T(8,128)(2,1)} %param.7, pred[32,1024]{1,0:T(8,128)(4,1)S(1)} %broadcast_compare_fusion, bf16[32,1024,1]{1,0,2:T(8,128)(2,1)S(1)} %select_bitcast_fusion), kind=kOutput, calls=%fused_computation.6 | convolution fusion | flops 12582912 | bytes 8503296 | tf_op jit(solution)/shard_map/roi,ro->ri/dot_general | solution.py:63
  17.4 5.5 collective-permute-start.3
  22.9 6.6 %broadcast_select_fusion.10 = bf16[32,1024,128]{2,1,0:T(8,128)(2,1)} fusion(bf16[32,1024,128]{2,1,0:T(8,128)(2,1)S(1)} %bitcast.90, pred[32,1024]{1,0:T(8,128)(4,1)S(1)} %broadcast_compare_fusion), kind=kLoop, calls=%fused_computation.5.clone.1.clone.clone.clone.2 | loop fusion | flops 4194304 | bytes 16809984 | tf_op jit(solution)/shard_map/roi,roj->rij/dot_general | solution.py:62
  29.5 8.3 %fusion.28 = bf16[32,128,128]{2,1,0:T(8,128)(2,1)S(1)} fusion(bf16[32,1024,128]{2,1,0:T(8,128)(2,1)} %broadcast_select_fusion.10), kind=kOutput, calls=%fused_computation.47 | convolution fusion | flops 1074266112 | bytes 9437184 | tf_op jit(solution)/shard_map/roi,roj->rij/dot_general | solution.py:62
  37.9 4.5 collective-permute-start.1
  42.7 0.1 reshape.630
  42.8 0.1 fusion.63
  42.9 0.1 copy.71
  43.0 0.1 compare_and_fusion
  43.1 0.1 compare_and_fusion.1
  43.2 0.1 compare_and_fusion.2
  43.3 0.1 compare_and_fusion.3
  43.4 11.2 %collective-permute-done.1 = bf16[32,128,128]{2,1,0:T(8,128)(2,1)S(1)} collective-permute-done((bf16[32,128,128]{2,1,0:T(8,128)(2,1)S(1)}, bf16[32,128,128]{2,1,0:T(8,128)(2,1)S(1)}, u32[]{:S(2)}, u32[]{:S(2)}) %collective-permute-start.1) | collective-permute-done | bytes 1048608 | tf_op jit(solution)/shard_map/ppermute | solution.py:15
  54.7 1.0 copy-done.12
  55.6 3.8 collective-permute-done
  59.5 2.0 pad_maximum_fusion
  61.5 7.7 %gather_fusion = bf16[160,128,128]{2,1,0:T(8,128)(2,1)} fusion(bf16[96,128,128]{2,1,0:T(8,128)(2,1)S(1)} %pad_maximum_fusion, s32[1024]{0:T(1024)S(1)} %pad_clamp_fusion), kind=kCustom, calls=%fused_computation | custom fusion | bytes 10486400 | tf_op jit(solution)/shard_map/gather | solution.py:69
  69.3 4.1 multiply_reduce_fusion
  73.3 1.3 copy.60
  74.7 0.1 compare_and_fusion.4
  74.8 0.1 compare_and_fusion.5
  74.9 0.1 copy.63
  75.0 0.1 copy.39
  75.2 0.8 gather_fusion.2
  75.9 0.3 fusion.98
  76.2 5.2 psum.15
  81.4 36.6 %all-reduce.2.cloned.1.call-done = bf16[32,128,128]{1,2,0:T(8,128)(2,1)} async-done(((bf16[32,128,128]{1,2,0:T(8,128)(2,1)}), bf16[32,128,128]{1,2,0:T(8,128)(2,1)}) %all-reduce.2.cloned.1.call-update) | async-done | bytes 1048592 | tf_op jit(solution)/shard_map/psum | solution.py:73
  118.0 1.5 convert_add_fusion
  119.5 1.8 copy.42
  121.3 3.3 fusion.12
  124.6 375.8 %custom-call.4 = f32[32,128,128]{2,1,0:T(8,128)S(1)} custom-call(f32[32,128,128]{2,1,0:T(8,128)} %fusion.12), custom_call_target="Cholesky" | custom-call | tf_op jit(solution)/shard_map/jit(cholesky)/cholesky | solution.py:44
  500.4 0.2 select_reduce_fusion
  500.6 1.1 copy-done.8
  501.7 0.1 compare_reduce_fusion
  501.8 1.9 select_select_fusion
  503.7 4.7 copy.43
  508.4 1.8 gather_fusion.1
  510.2 2.3 fusion.7
  512.6 3.6 fusion.5
  516.2 3.3 copy.46
  519.5 4.1 fusion.23
  523.6 3.9 fusion.26
  527.5 3.0 copy.47
  530.4 3.9 fusion.21
  534.4 3.6 fusion.93
  538.0 3.0 copy.48
  541.0 3.9 fusion.19
  544.9 3.6 fusion.94
  548.6 3.0 copy.49
  551.7 3.9 fusion.17
  555.6 3.6 fusion.95
  559.2 2.9 copy.50
  562.2 3.9 fusion.15
  566.1 3.5 fusion.96
  569.6 2.3 fusion.13
  572.0 3.6 fusion.97
  575.6 1.8 copy.51
  577.4 3.2 copy.52
  580.6 3.5 convolution_bitcast_fusion
  584.1 2.0 fusion.59
  586.1 10.8 %fusion.2 = bf16[32,512,128]{1,2,0:T(8,128)(2,1)} fusion(f32[32,512]{1,0:T(8,128)S(1)} %copy-done.13, bf16[32,512,128]{2,1,0:T(8,128)(2,1)} %param.12, f32[32,128,128]{1,2,0:T(8,128)} %copy.52, f32[32,128,128]{1,2,0:T(8,128)} %copy.51, f32[32,128,128]{1,2,0:T(8,128)} %copy.50, f32[32,128,128]{1,2,0:T(8,128)} %copy.49, f32[32,128,128]{1,2,0:T(8,128)} %copy.48, ...), kind=kOutput, calls=%fused_computation.8 | convolution fusion | flops 546832384 | bytes 23183360 | tf_op jit(solution)/shard_map/rpk,rkj->rpj/dot_general | solution.py:77
  596.8 6.4 %copy.54 = bf16[32,512,128]{2,1,0:T(8,128)(2,1)} copy(bf16[32,512,128]{1,2,0:T(8,128)(2,1)} %fusion.2) | data formatting | bytes 8388608 | tf_op jit(solution)/shard_map/convert_element_type | solution.py:78
  (70 shorter events, 0.5 us)
Async XLA Ops:
  6.5 111.4 %all-reduce.2.cloned.1.call-start = ((), (), s32[]{:S(2)}) async-start(), calls=%async_computation | async-start | bytes 2097152 | tf_op jit(solution)/shard_map/psum | solution.py:73
  7.3 15.6 %slice-start = ((s8[8388608]{0:T(1024)(128)(4,1)}), s8[4194304]{0:T(1024)(128)(4,1)S(1)}, s32[]{:S(2)}) async-start(s8[8388608]{0:T(1024)(128)(4,1)} %bitcast.89), calls=%async_computation.1 | async-start | bytes 8388608
  8.4 14.5 %slice-start.1 = ((s8[8388608]{0:T(1024)(128)(4,1)}), s8[4194304]{0:T(1024)(128)(4,1)S(1)}, s32[]{:S(2)}) async-start(s8[8388608]{0:T(1024)(128)(4,1)} %bitcast.89), calls=%async_computation.2 | async-start | bytes 8388608
  17.4 57.7 %collective-permute-start.3 = (bf16[32,128]{1,0:T(8,128)(2,1)S(1)}, bf16[32,128]{1,0:T(8,128)(2,1)S(1)}, u32[]{:S(2)}, u32[]{:S(2)}) collective-permute-start(bf16[32,128]{1,0:T(8,128)(2,1)S(1)} %convert_element_type.31), channel_id=1, source_target_pairs={{2,0},{4,2},{6,4},{8,6},{10,8},{12,10},{14,12},{16,14},{18,16},{20... | collective-permute-start | bytes 24584 | tf_op jit(solution)/shard_map/ppermute | solution.py:15
  22.9 52.2 %collective-permute-start.2 = (bf16[32,128]{1,0:T(8,128)(2,1)S(1)}, bf16[32,128]{1,0:T(8,128)(2,1)S(1)}, u32[]{:S(2)}, u32[]{:S(2)}) collective-permute-start(bf16[32,128]{1,0:T(8,128)(2,1)S(1)} %convert_element_type.31), channel_id=1, source_target_pairs={{0,2},{2,4},{4,6},{6,8},{8,10},{10,12},{12,14},{14,16},{16,18},{18... | collective-permute-start | bytes 24584 | tf_op jit(solution)/shard_map/ppermute | solution.py:14
  29.5 13.0 %copy-start.15 = (s32[32,5]{0,1:T(8,128)S(1)}, s32[32,5]{0,1:T(8,128)}, u32[]{:S(2)}) copy-start(s32[32,5]{0,1:T(8,128)} %param.10) | copy-start | bytes 1924
  29.5 13.4 %copy-start.14 = (f32[32,5]{0,1:T(8,128)S(1)}, f32[32,5]{0,1:T(8,128)}, u32[]{:S(2)}) copy-start(f32[32,5]{0,1:T(8,128)} %param.11) | copy-start | bytes 1924
  37.9 16.8 %copy-start.10 = (bf16[32,128,128]{2,1,0:T(8,128)(2,1)}, bf16[32,128,128]{2,1,0:T(8,128)(2,1)S(1)}, u32[]{:S(2)}) copy-start(bf16[32,128,128]{2,1,0:T(8,128)(2,1)S(1)} %fusion.28) | copy-start | bytes 3145732
  37.9 16.8 %collective-permute-start.1 = (bf16[32,128,128]{2,1,0:T(8,128)(2,1)S(1)}, bf16[32,128,128]{2,1,0:T(8,128)(2,1)S(1)}, u32[]{:S(2)}, u32[]{:S(2)}) collective-permute-start(bf16[32,128,128]{2,1,0:T(8,128)(2,1)S(1)} %fusion.28), channel_id=1, source_target_pairs={{2,0},{4,2},{6,4},{8,6},{10,8},{12,10},{14,12},{16,14},{18,16},{20... | collective-permute-start | bytes 3145736 | tf_op jit(solution)/shard_map/ppermute | solution.py:15
  42.4 17.1 %collective-permute-start = (bf16[32,128,128]{2,1,0:T(8,128)(2,1)S(1)}, bf16[32,128,128]{2,1,0:T(8,128)(2,1)}, u32[]{:S(2)}, u32[]{:S(2)}) collective-permute-start(bf16[32,128,128]{2,1,0:T(8,128)(2,1)S(1)} %fusion.28), channel_id=1, source_target_pairs={{0,2},{2,4},{4,6},{6,8},{8,10},{10,12},{12,14},{14,16},{16,18},{18... | collective-permute-start | bytes 3145736 | tf_op jit(solution)/shard_map/ppermute | solution.py:14
  54.7 1.0 copy-start.12
  119.5 1.8 copy-start.11
  500.4 1.3 copy-start.8
  519.5 4.1 copy-start.3
  530.4 3.9 copy-start.4
  541.0 3.9 copy-start.5
  551.6 4.0 copy-start.6
  562.1 3.9 copy-start.7
  569.6 2.3 copy-start
  571.9 3.6 copy-start.9
  577.4 3.2 copy-start.1
  580.6 3.5 copy-start.2
  584.1 2.0 copy-start.13
Sparse Core Ops, SparseCore 0:
  74.8 43.1 all-reduce.1
where the time goes:
time: 618 us; the launch traced here: 610 us
  other arithmetic  398 us (64%)
  matrix products  83.8 us (14%)
  waiting for transfers between devices  51.7 us (8%)
  local copies, waits for them, and re-layouts  47.4 us (8%)
  between operations  14.2 us (2%)
  starting transfers between devices  9.99 us (2%)
    another operation x3, other arithmetic, solve_region(): lower = jnp.linalg.cholesky(precision_mat)  376 us
    psum x1, waiting for transfers between devices, body(): lax.psum(local_gram.astype(jnp.bfloat16), 'obs').astype(jnp.float32)  36.6 us
    dot_general x7, matrix products, lower_inverse(): jnp.einsum('bij,bjk->bik', inverse, inner, precision=lax.Precision.HIGHEST)  25.6 us
    dot_general x7, matrix products, lower_inverse(): jnp.einsum('bij,bjk->bik', corner, inverse, precision=lax.Precision.HIGHEST)  24.4 us
    dot_general x7, local copies, waits for them, and re-layouts, lower_inverse(): jnp.einsum('bij,bjk->bik', inverse, inner, precision=lax.Precision.HIGHEST)  20.2 us
  transfers between devices with their start and end apart: 5, of which 3 were waited for; matrix products, arithmetic and copies ran while one was open for 5% of the time, Pallas kernels for 0%

commit v1 on v0

v1 whole, which is shorter than its diff:
```python
import functools

import jax
import jax.numpy as jnp
from jax import lax
from jax.experimental import pallas as pl
from jax.experimental.pallas import tpu as pltpu
from jax.sharding import PartitionSpec as P

MESH = pl.DeviceIdType.MESH
MEMBERS = 128
ROWS = MEMBERS + 16
PANEL = 16
LAG = 3
F32 = jnp.float32
BF16 = jnp.bfloat16


def dot_rows(left, right):
    return lax.dot_general(left, right, (((0,), (0,)), ((), ())), preferred_element_type=F32)


def iotas(shape):
    row = lax.broadcasted_iota(jnp.int32, shape, len(shape) - 2)
    col = lax.broadcasted_iota(jnp.int32, shape, len(shape) - 1)
    return row, col


def gram_kernel(
    n_region, y_hbm, d_ref, count_ref, gath, ybuf, dbuf, part, recv,
    y_sem, xs_sem, xr_sem, ups_sem, upr_sem, dns_sem, dnr_sem,
):
    pairs, _, slots, _ = ybuf.shape
    x = lax.axis_index("obs")
    me = lax.axis_index("region")
    partner = {"obs": 1 - x}
    right = {"region": lax.rem(me + 1, n_region)}
    left = {"region": lax.rem(me + n_region - 1, n_region)}

    def fetch(p):
        return pltpu.make_async_copy(y_hbm.at[pl.ds(2 * p, 2)], ybuf.at[p], y_sem.at[p])

    def swap(p):
        return pltpu.make_async_remote_copy(
            src_ref=part.at[p], dst_ref=recv.at[p], send_sem=xs_sem.at[p], recv_sem=xr_sem.at[p],
            device_id=partner, device_id_type=MESH,
        )

    def up(q):
        return pltpu.make_async_remote_copy(
            src_ref=gath.at[pairs + q], dst_ref=gath.at[q], send_sem=ups_sem.at[q],
            recv_sem=upr_sem.at[q], device_id=right, device_id_type=MESH,
        )

    def down(q):
        return pltpu.make_async_remote_copy(
            src_ref=gath.at[pairs + q], dst_ref=gath.at[2 * pairs + q], send_sem=dns_sem.at[q],
            recv_sem=dnr_sem.at[q], device_id=left, device_id_type=MESH,
        )

    def each(first, last, step):
        lax.fori_loop(first, last, lambda i, c: (step(i), c)[1], 0)

    each(0, pairs, lambda p: fetch(p).start())
    barrier = pltpu.get_barrier_semaphore()
    for other in (partner, left, right):
        pl.semaphore_signal(barrier, inc=1, device_id=other, device_id_type=MESH)
    dbuf[...] = d_ref[...].astype(F32)
    pl.semaphore_wait(barrier, 3)

    row, col = iotas((MEMBERS, MEMBERS))
    ext_row, _ = iotas((ROWS - MEMBERS, MEMBERS))
    slot_row, _ = iotas((slots, MEMBERS))
    slot_lane = lax.broadcasted_iota(jnp.int32, (1, slots), 1)

    def grams(p):
        fetch(p).wait()
        found = []
        for i in range(2):
            live = count_ref[2 * p + i] - x * slots
            y = ybuf[p, i]
            masked = jnp.where(slot_row < live, y, jnp.zeros((), BF16))
            d = jnp.where(slot_lane < live, dbuf[pl.ds(2 * p + i, 1), :], 0.0).astype(BF16)
            found.append((dot_rows(masked, y), jnp.dot(d, y, preferred_element_type=F32)))
        (gram0, proj0), (gram1, proj1) = found
        part[p, :MEMBERS] = jnp.where(row <= col, gram0, gram1).astype(BF16)
        diag = jnp.sum(jnp.where(row == col, gram1, 0.0), axis=0, keepdims=True)
        ext = jnp.where(ext_row == 0, diag, jnp.where(ext_row == 1, proj0, jnp.where(ext_row == 2, proj1, 0.0)))
        part[p, MEMBERS:] = ext.astype(BF16)
        swap(p).start()

    def forward(q):
        swap(q).wait_recv()
        gath[pairs + q] = (part[q].astype(F32) + recv[q].astype(F32)).astype(BF16)
        up(q).start()
        down(q).start()

    each(0, LAG, grams)

    def both(p):
        grams(p)
        forward(p - LAG)

    each(LAG, pairs, both)
    each(pairs - LAG, pairs, forward)

    def finish(q):
        swap(q).wait_send()
        up(q).wait()
        down(q).wait()

    each(0, pairs, finish)


def solve_kernel(
    place_ref, taper_ref, gath, par_hbm, mean_ref, out_hbm, mat, proj, pmt, parbuf, outbuf, in_sem, out_sem
):
    regions = mat.shape[0]
    near = taper_ref.shape[0] // regions

    def fetch(g):
        return pltpu.make_async_copy(par_hbm.at[g], parbuf.at[g], in_sem.at[g])

    def put(g):
        return pltpu.make_async_copy(outbuf.at[g], out_hbm.at[g], out_sem.at[g])

    def each(first, last, step, unroll=1):
        lax.fori_loop(first, last, lambda i, c: (step(i), c)[1], 0, unroll=unroll)

    each(0, regions, lambda g: fetch(g).start())

    pm = mean_ref[...]
    high = pm.astype(BF16).astype(F32)
    mid = (pm - high).astype(BF16).astype(F32)
    low = pm - high - mid
    pad = jnp.zeros((MEMBERS - 3 * regions, pm.shape[1]), F32)
    pmt[...] = jnp.concatenate([high, mid, low, pad], axis=0).T.astype(BF16)

    row, col = iotas((MEMBERS, MEMBERS))
    upper = row <= col
    diagonal = row == col

    def combine(g):
        acc = jnp.zeros((MEMBERS, MEMBERS), F32)
        ext = jnp.zeros((ROWS - MEMBERS, MEMBERS), F32)
        ext_row, _ = iotas((ROWS - MEMBERS, MEMBERS))
        for k in range(near):
            place = place_ref[g * near + k]
            weight = taper_ref[g * near + k]
            odd = place % 2
            even_w = jnp.where(odd == 0, weight, 0.0)
            odd_w = jnp.where(odd == 0, 0.0, weight)
            tile = gath[place // 2].astype(F32)
            acc = acc + jnp.where(upper, even_w, odd_w) * tile[:MEMBERS]
            ext = ext + jnp.where(ext_row == 1, even_w, odd_w) * tile[MEMBERS:]
        other = jnp.where(diagonal, ext[0:1] + (MEMBERS - 1.0), acc.T)
        mat[g] = acc + other
        proj[g] = jnp.broadcast_to(ext[1:2] + ext[2:3], (8, MEMBERS))

    each(0, regions, combine, 2)

    half = PANEL // 2
    h_row, h_lane = iotas((regions, half, MEMBERS))
    p_row, p_lane = iotas((PANEL, MEMBERS))

    def panel(p):
        start = pl.multiple_of(p * PANEL, PANEL)
        slab = mat[:, pl.ds(start, PANEL), :].reshape(regions * PANEL, MEMBERS)
        slab = pltpu.roll(slab, lax.rem(MEMBERS - start, MEMBERS), 1).reshape(regions, PANEL, MEMBERS)
        top, bot = slab[:, :half], slab[:, half:]
        inv_top = jnp.zeros((regions, half, MEMBERS), F32)
        inv_bot = jnp.zeros((regions, half, MEMBERS), F32)

        def shape(a):
            return jnp.broadcast_to(a, (regions, half, MEMBERS))

        for j in range(PANEL):
            i = j % half
            source = top if j < half else bot
            col_s = shape(source[:, :, j : j + 1])
            inv = 1.0 / shape(col_s[:, i : i + 1])
            pivot = jnp.where(h_lane == j, 1.0, shape(source[:, i : i + 1]))
            scaled = inv * pivot
            if j < half:
                inv_top = jnp.where(h_row == i, inv, inv_top)
                col_b = shape(bot[:, :, j : j + 1])
                below = h_row > i
                top = jnp.where((h_lane == j) & below, 0.0, top) - jnp.where(below, col_s, 0.0) * scaled
                bot = jnp.where(h_lane == j, 0.0, bot) - col_b * scaled
            else:
                inv_bot = jnp.where(h_row == i, inv, inv_bot)
                below = h_row > i
                bot = jnp.where((h_lane == j) & below, 0.0, bot) - jnp.where(below, col_s, 0.0) * scaled

        slab = jnp.concatenate([top, bot], axis=1)
        inv = jnp.concatenate([inv_top, inv_bot], axis=1)
        slab = pltpu.roll(slab.reshape(regions * PANEL, MEMBERS), start, 1).reshape(regions, PANEL, MEMBERS)
        mat[:, pl.ds(start, PANEL), :] = slab
        later = p_lane >= start + PANEL
        own = (p_lane >= start) & (p_lane < start + PANEL)
        strict = own & (p_lane - start > p_row)
        on_diag = own & (p_lane - start == p_row)
        clear = (row >= start + PANEL) & (col >= start) & (col < start + PANEL)
        for g in range(regions):
            factor = jnp.where(later, slab[g] * inv[g], 0.0)
            full = jnp.where(on_diag, 1.0, jnp.where(strict, 0.0, slab[g]))
            factor_h = factor.astype(BF16)
            factor_l = (factor - factor_h.astype(F32)).astype(BF16)
            full_h = full.astype(BF16)
            full_l = (full - full_h.astype(F32)).astype(BF16)
            update = dot_rows(
                jnp.concatenate([factor_h, factor_h, factor_l], axis=0),
                jnp.concatenate([full_h, full_l, full_h], axis=0),
            )
            mat[g] = jnp.where(clear, 0.0, mat[g]) - update

    each(0, MEMBERS // PANEL, panel)

    def apply(g):
        a = mat[g]
        pivots = jnp.sum(jnp.where(diagonal, a, 0.0), axis=1, keepdims=True)
        inverse = lax.rsqrt(pivots) * jnp.where(diagonal, 1.0, jnp.where(row > col, a, 0.0))
        step = jnp.sum(inverse * proj[g, 0:1, :], axis=1, keepdims=True)
        mean_weight = jnp.sum(inverse * step, axis=0, keepdims=True)
        transform = (mean_weight + (MEMBERS - 1.0) ** 0.5 * inverse).astype(BF16)
        pick = (col == g) | (col == regions + g) | (col == 2 * regions + g)
        ones = jnp.where(pick, 1.0, 0.0).astype(BF16)
        fetch(g).wait()
        moved = lax.dot_general(
            jnp.concatenate([parbuf[g], pmt[...]], axis=1),
            jnp.concatenate([transform, ones], axis=1),
            (((1,), (1,)), ((), ())),
            preferred_element_type=F32,
        )
        outbuf[g] = moved.astype(BF16)
        put(g).start()

    each(0, regions, apply, 2)
    each(0, regions, lambda g: put(g).wait())


def body(n_region, obs_anomaly, innovation, obs_count, neighbour, taper, param_anomaly, param_mean):
    regions, slots, _ = obs_anomaly.shape
    pars = param_anomaly.shape[1]
    pairs = regions // 2
    vmem = pl.BlockSpec(memory_space=pltpu.VMEM)
    smem = pl.BlockSpec(memory_space=pltpu.SMEM)
    hbm = pl.BlockSpec(memory_space=pl.ANY)
    gath = pl.pallas_call(
        functools.partial(gram_kernel, n_region),
        out_shape=jax.ShapeDtypeStruct((3 * pairs, ROWS, MEMBERS), BF16),
        in_specs=[hbm, vmem, smem],
        out_specs=vmem,
        scratch_shapes=[
            pltpu.VMEM((pairs, 2, slots, MEMBERS), BF16),
            pltpu.VMEM((regions, slots), F32),
            pltpu.VMEM((pairs, ROWS, MEMBERS), BF16),
            pltpu.VMEM((pairs, ROWS, MEMBERS), BF16),
        ]
        + [pltpu.SemaphoreType.DMA((pairs,))] * 7,
        compiler_params=pltpu.CompilerParams(
            collective_id=0, has_side_effects=True, vmem_limit_bytes=40 * 2**20
        ),
    )(obs_anomaly, innovation, obs_count)

    total = regions * n_region
    first = lax.axis_index("region") * regions
    place = (neighbour - first + regions) % total
    return pl.pallas_call(
        solve_kernel,
        out_shape=jax.ShapeDtypeStruct((regions, pars, MEMBERS), BF16),
        in_specs=[smem, smem, vmem, hbm, vmem],
        out_specs=hbm,
        scratch_shapes=[
            pltpu.VMEM((regions, MEMBERS, MEMBERS), F32),
            pltpu.VMEM((regions, 8, MEMBERS), F32),
            pltpu.VMEM((pars, MEMBERS), BF16),
            pltpu.VMEM((regions, pars, MEMBERS), BF16),
            pltpu.VMEM((regions, pars, MEMBERS), BF16),
            pltpu.SemaphoreType.DMA((regions,)),
            pltpu.SemaphoreType.DMA((regions,)),
        ],
        compiler_params=pltpu.CompilerParams(vmem_limit_bytes=40 * 2**20),
    )(place.reshape(-1), taper.reshape(-1), gath, param_anomaly, param_mean)


def solution(mesh):
    in_specs = (
        P("region", "obs", None),
        P("region", "obs"),
        P("region"),
        P("region", None),
        P("region", None),
        P("region", "obs", None),
        P("region", "obs"),
    )
    out_specs = P("region", "obs", None)
    return jax.shard_map(
        functools.partial(body, mesh.shape["region"]),
        mesh=mesh, in_specs=in_specs, out_specs=out_specs, check_vma=False,
    )
```

time: 618 us -> 80.8 us (0.13); the launches traced: 610 us -> 80.6 us
  other arithmetic: 398 us -> 0.7 us
  matrix products: 83.8 us -> 0 us
  Pallas kernels: 0 us -> 73.9 us
  waiting for transfers between devices: 51.7 us -> 0 us
  local copies, waits for them, and re-layouts: 47.4 us -> 5.95 us
  between operations: 14.2 us -> 0.04 us
  starting transfers between devices: 9.99 us -> 0 us
    another operation x3 -> x0, other arithmetic: 376 us -> none  [solve_region(): lower = jnp.linalg.cholesky(precision_mat)]
    dot_general x20 -> x0, matrix products: 83.8 us -> none  [the longest x7 25.6 us: lower_inverse(): jnp.einsum('bij,bjk->bik', inverse, inner, precision=lax.Precision.HIGHEST)]
    pallas_call x0 -> x2, Pallas kernels: none -> 73.9 us  [the longest x1 48 us: body(): pl.pallas_call(solve_kernel, out_shape=jax.ShapeDtypeStruct((regions, par...]
    psum x1 -> x0, waiting for transfers between devices: 36.6 us -> none  [body(): lax.psum(local_gram.astype(jnp.bfloat16), 'obs').astype(jnp.float32)]
    dot_general x8 -> x0, local copies, waits for them, and re-layouts: 21.5 us -> none  [the longest x7 20.2 us: lower_inverse(): jnp.einsum('bij,bjk->bik', inverse, inner, precision=lax.Precision.HIGHEST)]
    ppermute x4 -> x0, waiting for transfers between devices: 15.1 us -> none  [the longest x2 11.2 us: with_halo(): after = lax.ppermute(leading, axis, down)]
    gather x4 -> x0, local copies, waits for them, and re-layouts: 10.3 us -> none  [the longest x1 7.72 us: body(): wide_g[position]]
    ppermute x4 -> x0, starting transfers between devices: 9.98 us -> none  [the longest x2 9.98 us: with_halo(): after = lax.ppermute(leading, axis, down)]
  transfers between devices with their start and end apart: 5 -> 0, of which waited for: 3 -> 0; matrix products, arithmetic and copies ran while one was open for 5% -> 0% of each run, Pallas kernels for 0% -> 0%
where the time goes in v1:
time: 80.8 us; the launch traced here: 80.6 us
  Pallas kernels  73.9 us (91%)
  local copies, waits for them, and re-layouts  5.95 us (7%)
    pallas_call x1, Pallas kernels, body(): pl.pallas_call(solve_kernel, out_shape=jax.ShapeDtypeStruct((regions, par...  48 us
    pallas_call x1, Pallas kernels, body(): pl.pallas_call(functools.partial(gram_kernel, n_region), out_shape=jax.Sh...  25.9 us
    unnamed x11, local copies, waits for them, and re-layouts  5.65 us

profile of v1, /device:TPU:0, one launch (start us, length us, event | category | flops | bytes accessed | tf_op | source)
XLA Modules:
  0.0 80.6 jit_solution(17224334536225901047)
XLA Ops:
  0.0 0.7 add_select_fusion
  0.7 0.1 copy.8
  0.8 0.1 reshape.6.place_ref
  0.9 0.8 copy.9
  1.7 0.1 reshape.7.taper_ref
  1.8 0.0 copy-start
  1.8 3.4 %copy-done = bf16[32,1024,128]{2,1,0:T(8,128)(2,1)S(1)} copy-done((bf16[32,1024,128]{2,1,0:T(8,128)(2,1)S(1)}, bf16[32,1024,128]{2,1,0:T(8,128)(2,1)}, u32[]{:S(2)}) %copy-start) | copy-done | bytes 8388632
  5.2 0.0 copy-start.2
  5.2 0.8 %copy-done.2 = bf16[32,1024]{1,0:T(8,128)(2,1)S(1)} copy-done((bf16[32,1024]{1,0:T(8,128)(2,1)S(1)}, bf16[32,1024]{1,0:T(8,128)(2,1)}, u32[]{:S(2)}) %copy-start.2) | copy-done | bytes 65560
  6.0 0.0 copy-start.4
  6.0 0.7 copy-done.4
  6.7 0.0 copy-start.1
  6.7 0.0 copy-start.3
  6.7 25.9 %shard_map.73.gath = bf16[48,144,128]{2,1,0:T(8,128)(2,1)S(1)} custom-call(bf16[32,1024,128]{2,1,0:T(8,128)(2,1)S(1)} %copy-done, bf16[32,1024]{1,0:T(8,128)(2,1)S(1)} %copy-done.2, s32[32]{0:T(128)S(1)} %copy-done.4), custom_call_target="tpu_custom_call" | custom-call | tf_op jit(solution)/shard_map/pallas_call | solution.py:249
  32.6 0.0 copy-done.1
  32.6 0.0 copy-done.3
  32.6 48.0 %shard_map.74 = bf16[32,512,128]{2,1,0:T(8,128)(2,1)} custom-call(s32[160]{0:T(256)S(1)} %reshape.6.place_ref, f32[160]{0:T(256)S(1)} %reshape.7.taper_ref, bf16[48,144,128]{2,1,0:T(8,128)(2,1)S(1)} %shard_map.73.gath, bf16[32,512,128]{2,1,0:T(8,128)(2,1)S(1)} %copy-done.1, f32[32,512]{1,0:T(8,128)S(1)} %copy-done.3), custom_call_target="tpu_custom_call" | custom-call | tf_op jit(solution)/shard_map/pallas_call | solution.py:269
Async XLA Ops:
  1.8 3.4 %copy-start = (bf16[32,1024,128]{2,1,0:T(8,128)(2,1)S(1)}, bf16[32,1024,128]{2,1,0:T(8,128)(2,1)}, u32[]{:S(2)}) copy-start(bf16[32,1024,128]{2,1,0:T(8,128)(2,1)} %y_hbm.1) | copy-start | bytes 25165828
  5.2 0.8 %copy-start.2 = (bf16[32,1024]{1,0:T(8,128)(2,1)S(1)}, bf16[32,1024]{1,0:T(8,128)(2,1)}, u32[]{:S(2)}) copy-start(bf16[32,1024]{1,0:T(8,128)(2,1)} %d_ref.1) | copy-start | bytes 196612
  6.0 0.7 copy-start.4
  6.7 25.9 %copy-start.1 = (bf16[32,512,128]{2,1,0:T(8,128)(2,1)S(1)}, bf16[32,512,128]{2,1,0:T(8,128)(2,1)}, u32[]{:S(2)}) copy-start(bf16[32,512,128]{2,1,0:T(8,128)(2,1)} %par_hbm.1) | copy-start | bytes 12582916
  6.7 25.9 %copy-start.3 = (f32[32,512]{1,0:T(8,128)S(1)}, f32[32,512]{1,0:T(8,128)}, u32[]{:S(2)}) copy-start(f32[32,512]{1,0:T(8,128)} %mean_ref.1) | copy-start | bytes 196612

commit v2 on v1

--- a/solution.py
+++ b/solution.py
@@ -10,7 +10,7 @@
 MESH = pl.DeviceIdType.MESH
 MEMBERS = 128
 ROWS = MEMBERS + 16
-PANEL = 16
+PANEL = 8
 LAG = 3
 F32 = jnp.float32
 BF16 = jnp.bfloat16
@@ -113,10 +113,11 @@
 
 
 def solve_kernel(
-    place_ref, taper_ref, gath, par_hbm, mean_ref, out_hbm, mat, proj, pmt, parbuf, outbuf, in_sem, out_sem
+    total, near_ref, taper_ref, gath, par_hbm, mean_ref, out_hbm, mat, proj, pmt, parbuf, outbuf, in_sem, out_sem
 ):
     regions = mat.shape[0]
-    near = taper_ref.shape[0] // regions
+    near = taper_ref.shape[0]
+    before = total + regions - lax.axis_index("region") * regions
 
     def fetch(g):
         return pltpu.make_async_copy(par_hbm.at[g], parbuf.at[g], in_sem.at[g])
@@ -145,8 +146,8 @@
         ext = jnp.zeros((ROWS - MEMBERS, MEMBERS), F32)
         ext_row, _ = iotas((ROWS - MEMBERS, MEMBERS))
         for k in range(near):
-            place = place_ref[g * near + k]
-            weight = taper_ref[g * near + k]
+            place = lax.rem(near_ref[k, g] + before, total)
+            weight = taper_ref[k, g]
             odd = place % 2
             even_w = jnp.where(odd == 0, weight, 0.0)
             odd_w = jnp.where(odd == 0, 0.0, weight)
@@ -159,67 +160,48 @@
 
     each(0, regions, combine, 2)
 
-    half = PANEL // 2
-    h_row, h_lane = iotas((regions, half, MEMBERS))
+    h_row, h_lane = iotas((regions, PANEL, MEMBERS))
     p_row, p_lane = iotas((PANEL, MEMBERS))
 
-    def panel(p):
+    def shape(a):
+        return jnp.broadcast_to(a, (regions, PANEL, MEMBERS))
+
+    def panel(base, p):
         start = pl.multiple_of(p * PANEL, PANEL)
         slab = mat[:, pl.ds(start, PANEL), :].reshape(regions * PANEL, MEMBERS)
         slab = pltpu.roll(slab, lax.rem(MEMBERS - start, MEMBERS), 1).reshape(regions, PANEL, MEMBERS)
-        top, bot = slab[:, :half], slab[:, half:]
-        inv_top = jnp.zeros((regions, half, MEMBERS), F32)
-        inv_bot = jnp.zeros((regions, half, MEMBERS), F32)
-
-        def shape(a):
-            return jnp.broadcast_to(a, (regions, half, MEMBERS))
-
         for j in range(PANEL):
-            i = j % half
-            source = top if j < half else bot
-            col_s = shape(source[:, :, j : j + 1])
-            inv = 1.0 / shape(col_s[:, i : i + 1])
-            pivot = jnp.where(h_lane == j, 1.0, shape(source[:, i : i + 1]))
-            scaled = inv * pivot
-            if j < half:
-                inv_top = jnp.where(h_row == i, inv, inv_top)
-                col_b = shape(bot[:, :, j : j + 1])
-                below = h_row > i
-                top = jnp.where((h_lane == j) & below, 0.0, top) - jnp.where(below, col_s, 0.0) * scaled
-                bot = jnp.where(h_lane == j, 0.0, bot) - col_b * scaled
-            else:
-                inv_bot = jnp.where(h_row == i, inv, inv_bot)
-                below = h_row > i
-                bot = jnp.where((h_lane == j) & below, 0.0, bot) - jnp.where(below, col_s, 0.0) * scaled
-
-        slab = jnp.concatenate([top, bot], axis=1)
-        inv = jnp.concatenate([inv_top, inv_bot], axis=1)
+            col_j = shape(slab[:, :, j : j + 1])
+            root = lax.rsqrt(shape(col_j[:, j : j + 1]))
+            pivot = jnp.where(h_lane == j, 1.0, shape(slab[:, j : j + 1])) * root
+            factor = jnp.where(h_row > j, col_j * root, jnp.where(h_row == j, -1.0, 0.0))
+            drop = (h_row == j) | ((h_lane == j) & (h_row > j))
+            slab = jnp.where(drop, 0.0, slab) - factor * pivot
         slab = pltpu.roll(slab.reshape(regions * PANEL, MEMBERS), start, 1).reshape(regions, PANEL, MEMBERS)
         mat[:, pl.ds(start, PANEL), :] = slab
         later = p_lane >= start + PANEL
-        own = (p_lane >= start) & (p_lane < start + PANEL)
-        strict = own & (p_lane - start > p_row)
-        on_diag = own & (p_lane - start == p_row)
-        clear = (row >= start + PANEL) & (col >= start) & (col < start + PANEL)
+        strict = (p_lane < start + PANEL) & (p_lane - start > p_row)
+        clear = (row[base:] >= start + PANEL) & (col[base:] >= start) & (col[base:] < start + PANEL)
         for g in range(regions):
-            factor = jnp.where(later, slab[g] * inv[g], 0.0)
-            full = jnp.where(on_diag, 1.0, jnp.where(strict, 0.0, slab[g]))
-            factor_h = factor.astype(BF16)
-            factor_l = (factor - factor_h.astype(F32)).astype(BF16)
-            full_h = full.astype(BF16)
-            full_l = (full - full_h.astype(F32)).astype(BF16)
+            full = jnp.where(strict, 0.0, slab[g])
+            full_h = full.astype(BF16).astype(F32)
+            full_l = full - full_h
+            factor_h = jnp.where(later, full_h, 0.0)
+            factor_l = jnp.where(later, full_l, 0.0)
             update = dot_rows(
-                jnp.concatenate([factor_h, factor_h, factor_l], axis=0),
-                jnp.concatenate([full_h, full_l, full_h], axis=0),
+                jnp.concatenate([factor_h, factor_h, factor_l, factor_l], axis=0).astype(BF16),
+                jnp.concatenate([full_h, full_l, full_h, full_l], axis=0).astype(BF16),
             )
-            mat[g] = jnp.where(clear, 0.0, mat[g]) - update
-
-    each(0, MEMBERS // PANEL, panel)
+            mat[g, base:] = jnp.where(clear, 0.0, mat[g, base:]) - update[base:]
+
+    steps = MEMBERS // PANEL
+    parts = 4
+    for part in range(parts):
+        first, last = part * steps // parts, (part + 1) * steps // parts
+        each(first, last, functools.partial(panel, first * PANEL))
 
     def apply(g):
-        a = mat[g]
-        pivots = jnp.sum(jnp.where(diagonal, a, 0.0), axis=1, keepdims=True)
-        inverse = lax.rsqrt(pivots) * jnp.where(diagonal, 1.0, jnp.where(row > col, a, 0.0))
+        inverse = jnp.where(row >= col, mat[g], 0.0)
         step = jnp.sum(inverse * proj[g, 0:1, :], axis=1, keepdims=True)
         mean_weight = jnp.sum(inverse * step, axis=0, keepdims=True)
         transform = (mean_weight + (MEMBERS - 1.0) ** 0.5 * inverse).astype(BF16)
@@ -235,7 +217,7 @@
         outbuf[g] = moved.astype(BF16)
         put(g).start()
 
-    each(0, regions, apply, 2)
+    each(0, regions, apply, 4)
     each(0, regions, lambda g: put(g).wait())
 
 
@@ -245,7 +227,7 @@
     pairs = regions // 2
     vmem = pl.BlockSpec(memory_space=pltpu.VMEM)
     smem = pl.BlockSpec(memory_space=pltpu.SMEM)
-    hbm = pl.BlockSpec(memory_space=pl.ANY)
+    hbm = pl.BlockSpec(memory_space=pltpu.HBM)
     gath = pl.pallas_call(
         functools.partial(gram_kernel, n_region),
         out_shape=jax.ShapeDtypeStruct((3 * pairs, ROWS, MEMBERS), BF16),
@@ -263,11 +245,8 @@
         ),
     )(obs_anomaly, innovation, obs_count)
 
-    total = regions * n_region
-    first = lax.axis_index("region") * regions
-    place = (neighbour - first + regions) % total
     return pl.pallas_call(
-        solve_kernel,
+        functools.partial(solve_kernel, regions * n_region),
         out_shape=jax.ShapeDtypeStruct((regions, pars, MEMBERS), BF16),
         in_specs=[smem, smem, vmem, hbm, vmem],
         out_specs=hbm,
@@ -281,7 +260,7 @@
             pltpu.SemaphoreType.DMA((regions,)),
         ],
         compiler_params=pltpu.CompilerParams(vmem_limit_bytes=40 * 2**20),
-    )(place.reshape(-1), taper.reshape(-1), gath, param_anomaly, param_mean)
+    )(neighbour.T, taper.T, gath, param_anomaly, param_mean)
 
 
 def solution(mesh):

time: 80.8 us -> 79.6 us (0.985)
  local copies, waits for them, and re-layouts: 5.95 us -> 4.89 us
    unnamed x11 -> x14, local copies, waits for them, and re-layouts: 5.65 us -> 4.89 us
where the time goes in v2:
time: 79.6 us; the launch traced here: 79.4 us
  Pallas kernels  74.5 us (94%)
  local copies, waits for them, and re-layouts  4.89 us (6%)
    pallas_call x1, Pallas kernels, body(): pl.pallas_call(functools.partial(solve_kernel, regions * n_region), out_s...  48.5 us
    pallas_call x1, Pallas kernels, body(): pl.pallas_call(functools.partial(gram_kernel, n_region), out_shape=jax.Sh...  25.9 us
    unnamed x14, local copies, waits for them, and re-layouts  4.89 us

profile of v2, /device:TPU:0, one launch (start us, length us, event | category | flops | bytes accessed | tf_op | source)
XLA Modules:
  0.0 79.4 jit_solution(768043225677053975)
XLA Ops:
  0.0 0.0 copy-start
  0.0 3.4 %copy-done = bf16[32,1024,128]{2,1,0:T(8,128)(2,1)S(1)} copy-done((bf16[32,1024,128]{2,1,0:T(8,128)(2,1)S(1)}, bf16[32,1024,128]{2,1,0:T(8,128)(2,1)}, u32[]{:S(2)}) %copy-start) | copy-done | bytes 8388632
  3.4 0.0 copy-start.2
  3.4 0.8 %copy-done.2 = bf16[32,1024]{1,0:T(8,128)(2,1)S(1)} copy-done((bf16[32,1024]{1,0:T(8,128)(2,1)S(1)}, bf16[32,1024]{1,0:T(8,128)(2,1)}, u32[]{:S(2)}) %copy-start.2) | copy-done | bytes 65560
  4.2 0.0 copy-start.6
  4.2 0.7 copy-done.6
  4.9 0.0 copy-start.1
  4.9 0.0 copy-start.3
  4.9 0.0 copy-start.4
  4.9 0.0 copy-start.5
  4.9 25.9 %shard_map.73.gath = bf16[48,144,128]{2,1,0:T(8,128)(2,1)S(1)} custom-call(bf16[32,1024,128]{2,1,0:T(8,128)(2,1)S(1)} %copy-done, bf16[32,1024]{1,0:T(8,128)(2,1)S(1)} %copy-done.2, s32[32]{0:T(128)S(1)} %copy-done.6), custom_call_target="tpu_custom_call" | custom-call | tf_op jit(solution)/shard_map/pallas_call | solution.py:231
  30.8 0.0 copy-done.1
  30.8 0.0 copy-done.3
  30.8 0.0 copy-done.4
  30.9 0.0 copy-done.5
  30.9 48.5 %shard_map.74 = bf16[32,512,128]{2,1,0:T(8,128)(2,1)} custom-call(s32[5,32]{1,0:T(8,128)S(1)} %bitcast.2, f32[5,32]{1,0:T(8,128)S(1)} %bitcast.3, bf16[48,144,128]{2,1,0:T(8,128)(2,1)S(1)} %shard_map.73.gath, bf16[32,512,128]{2,1,0:T(8,128)(2,1)S(1)} %copy-done.1, f32[32,512]{1,0:T(8,128)S(1)} %copy-done.3), custom_call_target="tpu_custom_call" | custom-call | tf_op jit(solution)/shard_map/pallas_call | solution.py:248
Async XLA Ops:
  0.0 3.4 %copy-start = (bf16[32,1024,128]{2,1,0:T(8,128)(2,1)S(1)}, bf16[32,1024,128]{2,1,0:T(8,128)(2,1)}, u32[]{:S(2)}) copy-start(bf16[32,1024,128]{2,1,0:T(8,128)(2,1)} %y_hbm.1) | copy-start | bytes 25165828
  3.4 0.8 %copy-start.2 = (bf16[32,1024]{1,0:T(8,128)(2,1)S(1)}, bf16[32,1024]{1,0:T(8,128)(2,1)}, u32[]{:S(2)}) copy-start(bf16[32,1024]{1,0:T(8,128)(2,1)} %d_ref.1) | copy-start | bytes 196612
  4.2 0.7 copy-start.6
  4.9 26.0 %copy-start.1 = (bf16[32,512,128]{2,1,0:T(8,128)(2,1)S(1)}, bf16[32,512,128]{2,1,0:T(8,128)(2,1)}, u32[]{:S(2)}) copy-start(bf16[32,512,128]{2,1,0:T(8,128)(2,1)} %par_hbm.1) | copy-start | bytes 12582916
  4.9 26.0 %copy-start.3 = (f32[32,512]{1,0:T(8,128)S(1)}, f32[32,512]{1,0:T(8,128)}, u32[]{:S(2)}) copy-start(f32[32,512]{1,0:T(8,128)} %mean_ref.1) | copy-start | bytes 196612
  4.9 26.0 %copy-start.4 = (s32[32,5]{0,1:T(8,128)S(1)}, s32[32,5]{0,1:T(8,128)}, u32[]{:S(2)}) copy-start(s32[32,5]{0,1:T(8,128)} %param.10) | copy-start | bytes 1924
  4.9 26.0 %copy-start.5 = (f32[32,5]{0,1:T(8,128)S(1)}, f32[32,5]{0,1:T(8,128)}, u32[]{:S(2)}) copy-start(f32[32,5]{0,1:T(8,128)} %param.11) | copy-start | bytes 1924

commit v3 on v2

--- a/solution.py
+++ b/solution.py
@@ -10,14 +10,12 @@
 MESH = pl.DeviceIdType.MESH
 MEMBERS = 128
 ROWS = MEMBERS + 16
-PANEL = 8
-LAG = 3
+PANEL = 16
+HALF = PANEL // 2
+LAG = 2
+GROUP = 2
 F32 = jnp.float32
 BF16 = jnp.bfloat16
-
-
-def dot_rows(left, right):
-    return lax.dot_general(left, right, (((0,), (0,)), ((), ())), preferred_element_type=F32)
 
 
 def iotas(shape):
@@ -70,39 +68,48 @@
 
     row, col = iotas((MEMBERS, MEMBERS))
     ext_row, _ = iotas((ROWS - MEMBERS, MEMBERS))
-    slot_row, _ = iotas((slots, MEMBERS))
     slot_lane = lax.broadcasted_iota(jnp.int32, (1, slots), 1)
 
-    def grams(p):
-        fetch(p).wait()
-        found = []
-        for i in range(2):
-            live = count_ref[2 * p + i] - x * slots
-            y = ybuf[p, i]
-            masked = jnp.where(slot_row < live, y, jnp.zeros((), BF16))
-            d = jnp.where(slot_lane < live, dbuf[pl.ds(2 * p + i, 1), :], 0.0).astype(BF16)
-            found.append((dot_rows(masked, y), jnp.dot(d, y, preferred_element_type=F32)))
-        (gram0, proj0), (gram1, proj1) = found
-        part[p, :MEMBERS] = jnp.where(row <= col, gram0, gram1).astype(BF16)
-        diag = jnp.sum(jnp.where(row == col, gram1, 0.0), axis=0, keepdims=True)
-        ext = jnp.where(ext_row == 0, diag, jnp.where(ext_row == 1, proj0, jnp.where(ext_row == 2, proj1, 0.0)))
-        part[p, MEMBERS:] = ext.astype(BF16)
-        swap(p).start()
-
-    def forward(q):
-        swap(q).wait_recv()
-        gath[pairs + q] = (part[q].astype(F32) + recv[q].astype(F32)).astype(BF16)
-        up(q).start()
-        down(q).start()
-
+    def gram(g, y):
+        live = jnp.where(slot_lane < count_ref[g] - x * slots, 1.0, 0.0).astype(BF16)
+        d = jnp.broadcast_to(dbuf[pl.ds(g, 1), :], (ROWS - MEMBERS, slots)).astype(BF16)
+        both = jnp.concatenate([y.T, d], axis=0) * live
+        found = jnp.dot(both, y, preferred_element_type=F32)
+        return found[:MEMBERS], found[MEMBERS : MEMBERS + 1]
+
+    def grams(s):
+        for i in range(GROUP):
+            fetch(s * GROUP + i).wait()
+        for i in range(GROUP):
+            p = s * GROUP + i
+            gram0, proj0 = gram(2 * p, ybuf[p, 0])
+            gram1, proj1 = gram(2 * p + 1, ybuf[p, 1])
+            part[p, :MEMBERS] = jnp.where(row <= col, gram0, gram1).astype(BF16)
+            diag = jnp.sum(jnp.where(row == col, gram1, 0.0), axis=0, keepdims=True)
+            ext = jnp.where(ext_row == 0, diag, jnp.where(ext_row == 1, proj0, jnp.where(ext_row == 2, proj1, 0.0)))
+            part[p, MEMBERS:] = ext.astype(BF16)
+        for i in range(GROUP):
+            swap(s * GROUP + i).start()
+
+    def forward(s):
+        for i in range(GROUP):
+            swap(s * GROUP + i).wait_recv()
+        for i in range(GROUP):
+            q = s * GROUP + i
+            gath[pairs + q] = (part[q].astype(F32) + recv[q].astype(F32)).astype(BF16)
+        for i in range(GROUP):
+            up(s * GROUP + i).start()
+            down(s * GROUP + i).start()
+
+    groups = pairs // GROUP
     each(0, LAG, grams)
 
-    def both(p):
-        grams(p)
-        forward(p - LAG)
-
-    each(LAG, pairs, both)
-    each(pairs - LAG, pairs, forward)
+    def both(s):
+        grams(s)
+        forward(s - LAG)
+
+    each(LAG, groups, both)
+    each(groups - LAG, groups, forward)
 
     def finish(q):
         swap(q).wait_send()
@@ -160,39 +167,67 @@
 
     each(0, regions, combine, 2)
 
-    h_row, h_lane = iotas((regions, PANEL, MEMBERS))
+    h_row, h_lane = iotas((regions, HALF, MEMBERS))
+    t_row, t_lane = iotas((HALF, MEMBERS))
     p_row, p_lane = iotas((PANEL, MEMBERS))
 
     def shape(a):
-        return jnp.broadcast_to(a, (regions, PANEL, MEMBERS))
+        return jnp.broadcast_to(a, (regions, HALF, MEMBERS))
+
+    def eliminate(part, offset):
+        for i in range(HALF):
+            j = offset + i
+            col_j = shape(part[:, :, j : j + 1])
+            root = lax.rsqrt(shape(col_j[:, i : i + 1]))
+            pivot = jnp.where(h_lane == j, 1.0, shape(part[:, i : i + 1])) * root
+            factor = jnp.where(h_row > i, col_j * root, jnp.where(h_row == i, -1.0, 0.0))
+            drop = (h_row == i) | ((h_lane == j) & (h_row > i))
+            part = jnp.where(drop, 0.0, part) - factor * pivot
+        return part
+
+    def below(top, bot):
+        for j in range(HALF):
+            pivot = jnp.broadcast_to(top[j : j + 1], (HALF, MEMBERS))
+            root = jnp.broadcast_to(top[j : j + 1, j : j + 1], (HALF, MEMBERS))
+            factor = jnp.broadcast_to(bot[:, j : j + 1], (HALF, MEMBERS)) * root
+            bot = jnp.where(t_lane == j, 0.0, bot) - factor * pivot
+        return bot
 
     def panel(base, p):
         start = pl.multiple_of(p * PANEL, PANEL)
         slab = mat[:, pl.ds(start, PANEL), :].reshape(regions * PANEL, MEMBERS)
         slab = pltpu.roll(slab, lax.rem(MEMBERS - start, MEMBERS), 1).reshape(regions, PANEL, MEMBERS)
-        for j in range(PANEL):
-            col_j = shape(slab[:, :, j : j + 1])
-            root = lax.rsqrt(shape(col_j[:, j : j + 1]))
-            pivot = jnp.where(h_lane == j, 1.0, shape(slab[:, j : j + 1])) * root
-            factor = jnp.where(h_row > j, col_j * root, jnp.where(h_row == j, -1.0, 0.0))
-            drop = (h_row == j) | ((h_lane == j) & (h_row > j))
-            slab = jnp.where(drop, 0.0, slab) - factor * pivot
+        top = eliminate(slab[:, :HALF], 0)
+        bot = jnp.stack([below(top[g], slab[g, HALF:]) for g in range(regions)])
+        bot = eliminate(bot, HALF)
+        slab = jnp.concatenate([top, bot], axis=1)
         slab = pltpu.roll(slab.reshape(regions * PANEL, MEMBERS), start, 1).reshape(regions, PANEL, MEMBERS)
         mat[:, pl.ds(start, PANEL), :] = slab
         later = p_lane >= start + PANEL
         strict = (p_lane < start + PANEL) & (p_lane - start > p_row)
         clear = (row[base:] >= start + PANEL) & (col[base:] >= start) & (col[base:] < start + PANEL)
-        for g in range(regions):
-            full = jnp.where(strict, 0.0, slab[g])
-            full_h = full.astype(BF16).astype(F32)
-            full_l = full - full_h
-            factor_h = jnp.where(later, full_h, 0.0)
-            factor_l = jnp.where(later, full_l, 0.0)
-            update = dot_rows(
-                jnp.concatenate([factor_h, factor_h, factor_l, factor_l], axis=0).astype(BF16),
-                jnp.concatenate([full_h, full_l, full_h, full_l], axis=0).astype(BF16),
+        zeros = jnp.zeros((4 * PANEL, MEMBERS), BF16)
+        for g in range(0, regions, 2):
+            left, right = [], []
+            for h in (g, g + 1):
+                full = jnp.where(strict, 0.0, slab[h])
+                full_h = full.astype(BF16).astype(F32)
+                full_l = full - full_h
+                factor_h = jnp.where(later, full_h, 0.0)
+                factor_l = jnp.where(later, full_l, 0.0)
+                left += [factor_h, factor_h, factor_l, factor_l]
+                right.append(jnp.concatenate([full_h, full_l, full_h, full_l], axis=0).astype(BF16))
+            turned = jnp.concatenate(left, axis=0).T[base:].astype(BF16)
+            blocks = jnp.concatenate(
+                [
+                    jnp.concatenate([right[0], zeros], axis=1),
+                    jnp.concatenate([zeros, right[1]], axis=1),
+                ],
+                axis=0,
             )
-            mat[g, base:] = jnp.where(clear, 0.0, mat[g, base:]) - update[base:]
+            update = jnp.dot(turned, blocks, preferred_element_type=F32)
+            mat[g, base:] = jnp.where(clear, 0.0, mat[g, base:]) - update[:, :MEMBERS]
+            mat[g + 1, base:] = jnp.where(clear, 0.0, mat[g + 1, base:]) - update[:, MEMBERS:]
 
     steps = MEMBERS // PANEL
     parts = 4
@@ -241,7 +276,7 @@
         ]
         + [pltpu.SemaphoreType.DMA((pairs,))] * 7,
         compiler_params=pltpu.CompilerParams(
-            collective_id=0, has_side_effects=True, vmem_limit_bytes=40 * 2**20
+            collective_id=0, has_side_effects=True, vmem_limit_bytes=60 * 2**20
         ),
     )(obs_anomaly, innovation, obs_count)
 
@@ -259,7 +294,7 @@
             pltpu.SemaphoreType.DMA((regions,)),
             pltpu.SemaphoreType.DMA((regions,)),
         ],
-        compiler_params=pltpu.CompilerParams(vmem_limit_bytes=40 * 2**20),
+        compiler_params=pltpu.CompilerParams(vmem_limit_bytes=60 * 2**20),
     )(neighbour.T, taper.T, gath, param_anomaly, param_mean)
 
 

time: 79.6 us -> 75.1 us (0.943)
  local copies, waits for them, and re-layouts: 4.89 us -> 0 us
    unnamed x14 -> x0, local copies, waits for them, and re-layouts: 4.89 us -> none
where the time goes in v3:
time: 75.1 us; the launch traced here: 74.9 us
  Pallas kernels  74.8 us (100%)
    pallas_call x1, Pallas kernels, body(): pl.pallas_call(functools.partial(solve_kernel, regions * n_region), out_s...  48.2 us
    pallas_call x1, Pallas kernels, body(): pl.pallas_call(functools.partial(gram_kernel, n_region), out_shape=jax.Sh...  26.6 us

profile of v3, /device:TPU:0, one launch (start us, length us, event | category | flops | bytes accessed | tf_op | source)
XLA Modules:
  0.0 74.9 jit_solution(10659166016291859157)
XLA Ops:
  0.0 26.6 %shard_map.73.gath = bf16[48,144,128]{2,1,0:T(8,128)(2,1)} custom-call(bf16[32,1024,128]{2,1,0:T(8,128)(2,1)} %y_hbm.1, bf16[32,1024]{1,0:T(8,128)(2,1)} %d_ref.1, s32[32]{0:T(128)} %count_ref.1), custom_call_target="tpu_custom_call" | custom-call | tf_op jit(solution)/shard_map/pallas_call | solution.py:266
  26.6 48.2 %shard_map.74 = bf16[32,512,128]{2,1,0:T(8,128)(2,1)} custom-call(s32[5,32]{1,0:T(8,128)} %bitcast.2, f32[5,32]{1,0:T(8,128)} %bitcast.3, bf16[48,144,128]{2,1,0:T(8,128)(2,1)} %shard_map.73.gath, bf16[32,512,128]{2,1,0:T(8,128)(2,1)} %par_hbm.1, f32[32,512]{1,0:T(8,128)} %mean_ref.1), custom_call_target="tpu_custom_call" | custom-call | tf_op jit(solution)/shard_map/pallas_call | solution.py:283

commit v4 on v3

--- a/solution.py
+++ b/solution.py
@@ -14,6 +14,7 @@
 HALF = PANEL // 2
 LAG = 2
 GROUP = 2
+BATCH = 4
 F32 = jnp.float32
 BF16 = jnp.bfloat16
 
@@ -148,24 +149,28 @@
     upper = row <= col
     diagonal = row == col
 
-    def combine(g):
-        acc = jnp.zeros((MEMBERS, MEMBERS), F32)
-        ext = jnp.zeros((ROWS - MEMBERS, MEMBERS), F32)
-        ext_row, _ = iotas((ROWS - MEMBERS, MEMBERS))
+    ext_row, _ = iotas((ROWS - MEMBERS, MEMBERS))
+
+    def combined(g):
+        acc, ext = 0.0, 0.0
         for k in range(near):
             place = lax.rem(near_ref[k, g] + before, total)
             weight = taper_ref[k, g]
-            odd = place % 2
-            even_w = jnp.where(odd == 0, weight, 0.0)
-            odd_w = jnp.where(odd == 0, 0.0, weight)
-            tile = gath[place // 2].astype(F32)
+            odd = lax.bitwise_and(place, 1)
+            odd_w = weight * odd.astype(F32)
+            even_w = weight - odd_w
+            tile = gath[lax.shift_right_logical(place, 1)].astype(F32)
             acc = acc + jnp.where(upper, even_w, odd_w) * tile[:MEMBERS]
             ext = ext + jnp.where(ext_row == 1, even_w, odd_w) * tile[MEMBERS:]
         other = jnp.where(diagonal, ext[0:1] + (MEMBERS - 1.0), acc.T)
-        mat[g] = acc + other
-        proj[g] = jnp.broadcast_to(ext[1:2] + ext[2:3], (8, MEMBERS))
-
-    each(0, regions, combine, 2)
+        return acc + other, jnp.broadcast_to(ext[1:2] + ext[2:3], (8, MEMBERS))
+
+    def combine(s):
+        for i, (matrix, vector) in enumerate([combined(s * BATCH + i) for i in range(BATCH)]):
+            mat[s * BATCH + i] = matrix
+            proj[s * BATCH + i] = vector
+
+    each(0, regions // BATCH, combine)
 
     h_row, h_lane = iotas((regions, HALF, MEMBERS))
     t_row, t_lane = iotas((HALF, MEMBERS))
@@ -235,24 +240,33 @@
         first, last = part * steps // parts, (part + 1) * steps // parts
         each(first, last, functools.partial(panel, first * PANEL))
 
-    def apply(g):
+    means = pmt[...]
+
+    def update_of(g):
         inverse = jnp.where(row >= col, mat[g], 0.0)
         step = jnp.sum(inverse * proj[g, 0:1, :], axis=1, keepdims=True)
         mean_weight = jnp.sum(inverse * step, axis=0, keepdims=True)
         transform = (mean_weight + (MEMBERS - 1.0) ** 0.5 * inverse).astype(BF16)
         pick = (col == g) | (col == regions + g) | (col == 2 * regions + g)
         ones = jnp.where(pick, 1.0, 0.0).astype(BF16)
-        fetch(g).wait()
-        moved = lax.dot_general(
-            jnp.concatenate([parbuf[g], pmt[...]], axis=1),
-            jnp.concatenate([transform, ones], axis=1),
-            (((1,), (1,)), ((), ())),
-            preferred_element_type=F32,
-        )
-        outbuf[g] = moved.astype(BF16)
-        put(g).start()
-
-    each(0, regions, apply, 4)
+        return jnp.concatenate([transform, ones], axis=1)
+
+    def apply(s):
+        for i in range(BATCH):
+            fetch(s * BATCH + i).wait()
+        weights = [update_of(s * BATCH + i) for i in range(BATCH)]
+        for i in range(BATCH):
+            moved = lax.dot_general(
+                jnp.concatenate([parbuf[s * BATCH + i], means], axis=1),
+                weights[i],
+                (((1,), (1,)), ((), ())),
+                preferred_element_type=F32,
+            )
+            outbuf[s * BATCH + i] = moved.astype(BF16)
+        for i in range(BATCH):
+            put(s * BATCH + i).start()
+
+    each(0, regions // BATCH, apply)
     each(0, regions, lambda g: put(g).wait())
 
 

time: 75.1 us -> 68.7 us (0.915)
  Pallas kernels: 74.8 us -> 68.3 us
    pallas_call x1, Pallas kernels: 48.2 us -> 41.8 us  [body(): pl.pallas_call(functools.partial(solve_kernel, regions * n_region), out_s...]
where the time goes in v4:
time: 68.7 us; the launch traced here: 68.5 us
  Pallas kernels  68.3 us (99%)
    pallas_call x1, Pallas kernels, body(): pl.pallas_call(functools.partial(solve_kernel, regions * n_region), out_s...  41.8 us
    pallas_call x1, Pallas kernels, body(): pl.pallas_call(functools.partial(gram_kernel, n_region), out_shape=jax.Sh...  26.6 us

profile of v4, /device:TPU:0, one launch (start us, length us, event | category | flops | bytes accessed | tf_op | source)
XLA Modules:
  0.0 68.5 jit_solution(16205394539186266620)
XLA Ops:
  0.0 26.6 %shard_map.73.gath = bf16[48,144,128]{2,1,0:T(8,128)(2,1)} custom-call(bf16[32,1024,128]{2,1,0:T(8,128)(2,1)} %y_hbm.1, bf16[32,1024]{1,0:T(8,128)(2,1)} %d_ref.1, s32[32]{0:T(128)} %count_ref.1), custom_call_target="tpu_custom_call" | custom-call | tf_op jit(solution)/shard_map/pallas_call | solution.py:280
  26.6 41.8 %shard_map.74 = bf16[32,512,128]{2,1,0:T(8,128)(2,1)} custom-call(s32[5,32]{1,0:T(8,128)} %bitcast.2, f32[5,32]{1,0:T(8,128)} %bitcast.3, bf16[48,144,128]{2,1,0:T(8,128)(2,1)} %shard_map.73.gath, bf16[32,512,128]{2,1,0:T(8,128)(2,1)} %par_hbm.1, f32[32,512]{1,0:T(8,128)} %mean_ref.1), custom_call_target="tpu_custom_call" | custom-call | tf_op jit(solution)/shard_map/pallas_call | solution.py:297

commit v5 on v4

--- a/solution.py
+++ b/solution.py
@@ -12,9 +12,9 @@
 ROWS = MEMBERS + 16
 PANEL = 16
 HALF = PANEL // 2
-LAG = 2
+LAG = 1
 GROUP = 2
-BATCH = 4
+BATCH = 8
 F32 = jnp.float32
 BF16 = jnp.bfloat16
 
@@ -180,14 +180,24 @@
         return jnp.broadcast_to(a, (regions, HALF, MEMBERS))
 
     def eliminate(part, offset):
-        for i in range(HALF):
+        for i in range(0, HALF, 2):
             j = offset + i
-            col_j = shape(part[:, :, j : j + 1])
-            root = lax.rsqrt(shape(col_j[:, i : i + 1]))
-            pivot = jnp.where(h_lane == j, 1.0, shape(part[:, i : i + 1])) * root
-            factor = jnp.where(h_row > i, col_j * root, jnp.where(h_row == i, -1.0, 0.0))
-            drop = (h_row == i) | ((h_lane == j) & (h_row > i))
-            part = jnp.where(drop, 0.0, part) - factor * pivot
+            col_0, col_1 = shape(part[:, :, j : j + 1]), shape(part[:, :, j + 1 : j + 2])
+            row_0, row_1 = shape(part[:, i : i + 1]), shape(part[:, i + 1 : i + 2])
+            root_0 = lax.rsqrt(shape(col_0[:, i : i + 1]))
+            factor_0 = col_0 * root_0
+            link = shape(factor_0[:, i + 1 : i + 2])
+            col_1 = col_1 - factor_0 * link
+            root_1 = lax.rsqrt(shape(col_1[:, i + 1 : i + 2]))
+            pivot_0 = jnp.where(h_lane == j, 1.0, row_0) * root_0
+            row_1 = jnp.where(h_lane == j, 0.0, row_1) - link * pivot_0
+            pivot_1 = jnp.where(h_lane == j + 1, 1.0, row_1) * root_1
+            factor_0 = jnp.where(h_row > i + 1, factor_0, jnp.where(h_row == i, -1.0, 0.0))
+            factor_1 = jnp.where(h_row > i + 1, col_1 * root_1, jnp.where(h_row == i + 1, -1.0, 0.0))
+            drop_0 = (h_row == i) | ((h_lane == j) & (h_row > i + 1))
+            drop_1 = (h_row == i + 1) | ((h_lane == j + 1) & (h_row > i + 1))
+            part = jnp.where(drop_0, 0.0, part) - factor_0 * pivot_0
+            part = jnp.where(drop_1, 0.0, part) - factor_1 * pivot_1
         return part
 
     def below(top, bot):

time: 68.7 us -> 66.2 us (0.964)
  Pallas kernels: 68.3 us -> 65.9 us
    pallas_call x1, Pallas kernels: 41.8 us -> 36.6 us  [body(): pl.pallas_call(functools.partial(solve_kernel, regions * n_region), out_s...]
    pallas_call x1, Pallas kernels: 26.6 us -> 29.3 us  [body(): pl.pallas_call(functools.partial(gram_kernel, n_region), out_shape=jax.Sh...]
where the time goes in v5:
time: 66.2 us; the launch traced here: 66.1 us
  Pallas kernels  65.9 us (100%)
    pallas_call x1, Pallas kernels, body(): pl.pallas_call(functools.partial(solve_kernel, regions * n_region), out_s...  36.6 us
    pallas_call x1, Pallas kernels, body(): pl.pallas_call(functools.partial(gram_kernel, n_region), out_shape=jax.Sh...  29.3 us

profile of v5, /device:TPU:0, one launch (start us, length us, event | category | flops | bytes accessed | tf_op | source)
XLA Modules:
  0.0 66.1 jit_solution(12475400643681338692)
XLA Ops:
  0.0 29.3 %shard_map.73.gath = bf16[48,144,128]{2,1,0:T(8,128)(2,1)} custom-call(bf16[32,1024,128]{2,1,0:T(8,128)(2,1)} %y_hbm.1, bf16[32,1024]{1,0:T(8,128)(2,1)} %d_ref.1, s32[32]{0:T(128)} %count_ref.1), custom_call_target="tpu_custom_call" | custom-call | tf_op jit(solution)/shard_map/pallas_call | solution.py:290
  29.3 36.6 %shard_map.74 = bf16[32,512,128]{2,1,0:T(8,128)(2,1)} custom-call(s32[5,32]{1,0:T(8,128)} %bitcast.2, f32[5,32]{1,0:T(8,128)} %bitcast.3, bf16[48,144,128]{2,1,0:T(8,128)(2,1)} %shard_map.73.gath, bf16[32,512,128]{2,1,0:T(8,128)(2,1)} %par_hbm.1, f32[32,512]{1,0:T(8,128)} %mean_ref.1), custom_call_target="tpu_custom_call" | custom-call | tf_op jit(solution)/shard_map/pallas_call | solution.py:307

commit v6 on v5

--- a/solution.py
+++ b/solution.py
@@ -12,7 +12,7 @@
 ROWS = MEMBERS + 16
 PANEL = 16
 HALF = PANEL // 2
-LAG = 1
+LAG = 2
 GROUP = 2
 BATCH = 8
 F32 = jnp.float32

time: 66.2 us -> 63.6 us (0.961)
  Pallas kernels: 65.9 us -> 63.2 us
    pallas_call x1, Pallas kernels: 29.3 us -> 26.6 us  [body(): pl.pallas_call(functools.partial(gram_kernel, n_region), out_shape=jax.Sh...]
where the time goes in v6:
time: 63.6 us; the launch traced here: 63.4 us
  Pallas kernels  63.2 us (99%)
    pallas_call x1, Pallas kernels, body(): pl.pallas_call(functools.partial(solve_kernel, regions * n_region), out_s...  36.6 us
    pallas_call x1, Pallas kernels, body(): pl.pallas_call(functools.partial(gram_kernel, n_region), out_shape=jax.Sh...  26.6 us

profile of v6, /device:TPU:0, one launch (start us, length us, event | category | flops | bytes accessed | tf_op | source)
XLA Modules:
  0.0 63.4 jit_solution(11962473296414953833)
XLA Ops:
  0.0 26.6 %shard_map.73.gath = bf16[48,144,128]{2,1,0:T(8,128)(2,1)} custom-call(bf16[32,1024,128]{2,1,0:T(8,128)(2,1)} %y_hbm.1, bf16[32,1024]{1,0:T(8,128)(2,1)} %d_ref.1, s32[32]{0:T(128)} %count_ref.1), custom_call_target="tpu_custom_call" | custom-call | tf_op jit(solution)/shard_map/pallas_call | solution.py:290
  26.6 36.6 %shard_map.74 = bf16[32,512,128]{2,1,0:T(8,128)(2,1)} custom-call(s32[5,32]{1,0:T(8,128)} %bitcast.2, f32[5,32]{1,0:T(8,128)} %bitcast.3, bf16[48,144,128]{2,1,0:T(8,128)(2,1)} %shard_map.73.gath, bf16[32,512,128]{2,1,0:T(8,128)(2,1)} %par_hbm.1, f32[32,512]{1,0:T(8,128)} %mean_ref.1), custom_call_target="tpu_custom_call" | custom-call | tf_op jit(solution)/shard_map/pallas_call | solution.py:307
